TPU v7x, 32 devices: a whole 2x2x4 slice. The times are simulated.
32 devices in a mesh: groups: 2 (over x), ctx: 2 (over core), fsdp: 8 (over z, y).
Axes of the slice: x: 2, y: 2, z: 4, core: 2. Of those that a mesh axis runs over, the one named last changes fastest.
Arguments:
- hidden_in: bfloat16 [8192, 2048], P(('groups', 'ctx', 'fsdp')), parts along dimension 0, may hold values from -6 to 6
- qkv_weight: bfloat16 [2048, 4096], P(None, 'fsdp'), may hold values from -0.125 to 0.125
- ab_weight: bfloat16 [2048, 32], replicated, may hold values from -0.125 to 0.125
- conv_weight: float32 [4, 4096], replicated, may hold values from -3 to 3
- decay_rate: float32 [16], replicated, may hold values from 7.324219e-05 to 0.3
- dt_bias: float32 [16], replicated, may hold values from -3 to -1
- norm_gain: float32 [128], replicated, may hold values from 0.1 to 1.9
- previous_tail: bfloat16 [6, 4096], P('groups'), parts along dimension 0, may hold values from -6 to 6
- window_entry_state: float32 [32, 128, 128], P('groups'), parts along dimension 0, may hold values from -3 to 3
Outputs:
- head_out: bfloat16 [8192, 2048], P(('groups', 'ctx', 'fsdp')), parts along dimension 0
There are 2 independent parts, one for each index of `groups`. A program takes and returns all parts, laid end to end along the dimension named above; an argument that names none is the same for every part. Nothing has to cross between parts.
All inputs are finite; a program needn't handle non-finite values.
Results may differ from a plain program's by a relative error of at most 0.0065.
Values may be sent and summed in bfloat16 or wider, within the bound.
A program may use at most 320 MiB of HBM per device.

v0:
```python
import jax
import jax.numpy as jnp
from jax import lax
from jax.sharding import PartitionSpec as P

HK = 8
HV = 16
DK = 128
DV = 128
SPAN = 64
exact_product = lax.Precision.HIGHEST


def shifted(array, axis, by):
    peers = lax.axis_size(axis)
    pairs = [(i, i + by) for i in range(peers) if 0 <= i + by < peers]
    return lax.ppermute(array, axis, pairs)


def entering(part, axis, combine, identity):
    place = lax.axis_index(axis)
    gathered = jax.tree.map(lambda a: lax.all_gather(a, axis), part)
    state = jax.tree.map(lambda a, e: jnp.zeros_like(a) + jnp.asarray(e, a.dtype), part, identity)

    def one(hop, state):
        return combine(
            state, jax.tree.map(lambda a: lax.dynamic_index_in_dim(a, hop, 0, False), gathered)
        )

    return lax.fori_loop(0, place, one, state)


def unit_norm(vectors):
    return vectors * lax.rsqrt(jnp.sum(vectors * vectors, axis=-1, keepdims=True) + 1e-06)


def convolve(before, mixed_qkv, conv_weight):
    length = mixed_qkv.shape[0]
    padded = jnp.concatenate([before, mixed_qkv], axis=0).astype(jnp.float32)
    summed = jnp.zeros((length, mixed_qkv.shape[1]), jnp.float32)
    for offset in range(conv_weight.shape[0]):
        summed = summed + conv_weight[offset] * padded[offset : offset + length]
    return jax.nn.silu(summed)


def to_spans(tensor, span_len):
    length, head_count = (tensor.shape[0], tensor.shape[1])
    shaped = tensor.reshape((length // span_len, span_len, head_count) + tensor.shape[2:])
    return jnp.moveaxis(shaped, 2, 1)


def head_inputs(conv_out, gate_logits, decay_rate, dt_bias):
    length = conv_out.shape[0]
    queries = unit_norm(conv_out[:, : HK * DK].reshape(length, HK, DK)) * DK ** (-0.5)
    head_keys = unit_norm(conv_out[:, HK * DK : 2 * HK * DK].reshape(length, HK, DK))
    values = conv_out[:, 2 * HK * DK :].reshape(length, HV, DV)
    queries = jnp.repeat(queries, HV // HK, axis=1)
    head_keys = jnp.repeat(head_keys, HV // HK, axis=1)
    write_rate = jax.nn.sigmoid(gate_logits[:, HV:])
    logdecay = -decay_rate * jax.nn.softplus(gate_logits[:, :HV] + dt_bias)
    return [to_spans(item, SPAN) for item in (queries, head_keys, values, write_rate, logdecay)]


def lower_inverse(strict_part):
    span_len = strict_part.shape[-1]
    unit_span = jnp.eye(span_len, dtype=strict_part.dtype)
    inverse = unit_span - strict_part
    power = strict_part
    reach = 2
    while reach < span_len:
        power = jnp.einsum("...ij,...jk->...ik", power, power, precision=exact_product)
        inverse = inverse + jnp.einsum(
            "...ij,...jk->...ik", inverse, power, precision=exact_product
        )
        reach = reach * 2
    return inverse


def span_terms(queries, head_keys, values, write_rate, logdecay):
    span_len = logdecay.shape[-1]
    cumulative = jnp.cumsum(logdecay, axis=-1)
    row_index = lax.broadcasted_iota(jnp.int32, (span_len, span_len), 0)
    col_index = lax.broadcasted_iota(jnp.int32, (span_len, span_len), 1)
    lower_mask = row_index >= col_index
    gap_log = cumulative[..., :, None] - cumulative[..., None, :]
    factor = jnp.where(lower_mask, jnp.exp(jnp.where(lower_mask, gap_log, 0.0)), 0.0)
    strict = jnp.where(row_index > col_index, factor, 0.0)
    key_products = jnp.einsum("...ik,...jk->...ij", head_keys, head_keys, precision=exact_product)
    query_products = jnp.einsum("...ik,...jk->...ij", queries, head_keys, precision=exact_product)
    inverse = lower_inverse(write_rate[..., :, None] * key_products * strict)
    growth = jnp.exp(cumulative)
    right_sides = jnp.concatenate(
        [write_rate[..., None] * values, (write_rate * growth)[..., None] * head_keys], axis=-1
    )
    solved = jnp.einsum("...ij,...jc->...ic", inverse, right_sides, precision=exact_product)
    new_values = solved[..., : values.shape[-1]]
    key_weights = solved[..., values.shape[-1] :]
    scores = query_products * factor
    window_local_output = jnp.einsum(
        "...ij,...jv->...iv", scores, new_values, precision=exact_product
    )
    effective_query = growth[..., None] * queries - jnp.einsum(
        "...ij,...jk->...ik", scores, key_weights, precision=exact_product
    )
    span_end = cumulative[..., -1]
    tail_decay = jnp.exp(span_end[..., None] - cumulative)
    decayed_keys = head_keys * tail_decay[..., None]
    unit_key = jnp.eye(head_keys.shape[-1], dtype=logdecay.dtype)
    state_mapping = jnp.exp(span_end)[..., None, None] * unit_key - jnp.einsum(
        "...ck,...cj->...kj", decayed_keys, key_weights, precision=exact_product
    )
    shifted_state = jnp.einsum(
        "...ck,...cv->...kv", decayed_keys, new_values, precision=exact_product
    )
    return (effective_query, window_local_output, state_mapping, shifted_state)


def finish(result_rows, norm_gain):
    mean_square = jnp.mean(result_rows * result_rows, axis=-1, keepdims=True)
    normed = result_rows * lax.rsqrt(mean_square + 1e-06) * norm_gain
    normed = jnp.moveaxis(normed, 1, 2)
    return normed.reshape(
        normed.shape[0] * normed.shape[1], normed.shape[2] * normed.shape[3]
    ).astype(jnp.bfloat16)


def compose(former_piece, latter_piece):
    joined_map = jnp.einsum(
        "hkj,hjm->hkm", latter_piece[0], former_piece[0], precision=exact_product
    )
    combined_state = (
        jnp.einsum("zom,zmg->zog", latter_piece[0], former_piece[1], precision=exact_product)
        + latter_piece[1]
    )
    return (joined_map, combined_state)


def shards(
    hidden_in,
    qkv_weight,
    ab_weight,
    conv_weight,
    decay_rate,
    dt_bias,
    norm_gain,
    previous_tail,
    window_entry_state,
):
    mixed_qkv = jnp.dot(
        hidden_in,
        lax.all_gather(qkv_weight, "fsdp", axis=1, tiled=True),
        preferred_element_type=jnp.float32,
    ).astype(jnp.bfloat16)
    gate_logits = jnp.dot(hidden_in, ab_weight, preferred_element_type=jnp.float32)
    tail_rows = previous_tail.shape[0]
    received = shifted(mixed_qkv[mixed_qkv.shape[0] - tail_rows :], ("ctx", "fsdp"), 1)
    before = jnp.where(lax.axis_index(("ctx", "fsdp")) == 0, previous_tail, received)
    conv_out = convolve(before, mixed_qkv, conv_weight)
    spanned = head_inputs(conv_out, gate_logits, decay_rate, dt_bias)
    effective_query, window_local_output, state_mapping, shifted_state = span_terms(*spanned)
    unit_maps = jnp.broadcast_to(jnp.eye(DK, dtype=jnp.float32), (HV, DK, DK))
    empty_state = jnp.zeros((HV, DK, DV), jnp.float32)

    def advance(carried, items):
        carry_map, carried_over_state = carried
        per_step_query, per_step_local, per_step_mapping, step_offset = items
        adjusted_result = jnp.einsum(
            "hck,hkj->hcj", per_step_query, carry_map, precision=exact_product
        )
        layer_result = per_step_local + jnp.einsum(
            "gpi,gib->gpb", per_step_query, carried_over_state, precision=exact_product
        )
        carry_map = jnp.einsum("hkj,hjm->hkm", per_step_mapping, carry_map, precision=exact_product)
        carried_over_state = (
            jnp.einsum(
                "zom,zmg->zog", per_step_mapping, carried_over_state, precision=exact_product
            )
            + step_offset
        )
        return ((carry_map, carried_over_state), (adjusted_result, layer_result))

    own_pair, (adjusted_result, incomplete_output) = lax.scan(
        advance,
        (unit_maps, empty_state),
        (effective_query, window_local_output, state_mapping, shifted_state),
    )
    identity = (unit_maps, empty_state)
    leading_pair = entering((own_pair[0], own_pair[1]), ("ctx", "fsdp"), compose, identity)
    opening_state = (
        jnp.einsum("zom,zmg->zog", leading_pair[0], window_entry_state, precision=exact_product)
        + leading_pair[1]
    )
    result_rows = incomplete_output + jnp.einsum(
        "elfx,lxw->elfw", adjusted_result, opening_state, precision=exact_product
    )
    return finish(result_rows, norm_gain)


def solution(mesh):
    placed = (
        P(("groups", "ctx", "fsdp"), None),
        P(None, "fsdp"),
        P(),
        P(),
        P(),
        P(),
        P(),
        P("groups", None),
        P("groups", None, None),
    )
    return jax.shard_map(
        shards,
        mesh=mesh,
        in_specs=placed,
        out_specs=P(("groups", "ctx", "fsdp"), None),
        check_vma=False,
    )
```

profile of v0, /device:TPU:31, one launch (start us, length us, event | category | flops | bytes accessed | tf_op | source)
XLA Modules:
  0.0 710.3 jit_solution(9324896033051884628)
XLA Ops:
  9.7 225.8 %all-gather.6.cloned.1.call-done = bf16[2048,4096]{1,0:T(8,128)(2,1)} async-done(((bf16[2048,512]{1,0:T(8,128)(2,1)}), bf16[2048,4096]{1,0:T(8,128)(2,1)}) %all-gather.6.cloned.1.call-update) | async-done | bytes 16777232 | tf_op jit(solution)/shard_map/all_gather | solution.py:151
  235.5 8.4 %convolution_convert_fusion = bf16[256,4096]{1,0:T(8,128)(2,1)S(1)} fusion(bf16[256,2048]{1,0:T(8,128)(2,1)S(1)} %copy-done, bf16[2048,4096]{1,0:T(8,128)(2,1)} %all-gather.6.cloned.1.call-done), kind=kOutput, calls=%fused_computation.35 | convolution fusion | flops 4296015872 | bytes 19922944 | tf_op jit(solution)/shard_map/dot_general | solution.py:149
  246.5 3.0 collective-permute-done
  250.9 2.8 divide_multiply_fusion
  257.3 3.5 fusion.45
  260.8 3.6 select_multiply_fusion
  266.6 2.7 fusion.88
  289.3 4.5 fusion.34
  293.8 3.6 fusion.47
  297.4 3.9 fusion.40
  301.4 8.9 %fusion.46 = f32[4,16,128,128]{3,2,1,0:T(8,128)} fusion(f32[4,16,64,256]{3,2,1,0:T(8,128)S(1)} %fusion.34, f32[4,64,16,128]{3,1,0,2:T(8,128)S(1)} %bitcast.166, f32[4,16,64]{2,1,0:T(8,128)S(1)} %get-tuple-element.163), kind=kOutput, calls=%fused_computation.68 | convolution fusion | flops 805830656 | bytes 8421376 | tf_op jit(solution)/shard_map/...ck,...cv->...kv/dot_general | solution.py:112
  310.2 9.7 %multiply_subtract_fusion = f32[4,16,128,128]{3,2,1,0:T(8,128)} fusion(f32[128,128]{1,0:T(8,128)S(1)} %fusion.76, f32[4,16]{1,0:T(4,128)S(1)} %exp.36, f32[4,16,64,256]{3,2,1,0:T(8,128)S(1)} %fusion.34, f32[4,64,16,128]{3,1,0,2:T(8,128)S(1)} %bitcast.167, f32[4,16,64]{2,1,0:T(8,128)S(1)} %get-tuple-element.163), kind=kOutput, calls=%fused_computation.48 | convolution fusion | flops 807927808 | bytes 8488960 | tf_op jit(solution)/shard_map/...ck,...cj->...kj/dot_general | solution.py:109
  320.0 39.9 %while.30 = (s32[]{:T(128)}, f32[16,128,128]{2,1,0:T(8,128)S(1)}, f32[16,128,128]{2,1,0:T(8,128)S(1)}, f32[4,16,64,128]{3,2,0,1:T(8,128)}, f32[4,16,64,128]{3,2,...) while((s32[]{:T(128)}, f32[16,128,128]{2,1,0:T(8,128)S(1)}, ...), condition=%wide.region_4.5_spmd.clone, body=%wide.region_3.4_spmd.clone.sunk | while | flops 1208877056 | bytes 41423032 | solution.py:182
  324.7 2.9 fusion.157
  334.6 2.9 fusion.157
  344.6 2.9 fusion.157
  354.6 2.9 fusion.157
  361.7 126.7 %all-gather.8.cloned.1.call-done = f32[256,128,128]{2,1,0:T(8,128)} async-done(((f32[16,128,128]{2,1,0:T(8,128)}), f32[256,128,128]{2,1,0:T(8,128)}) %all-gather.8.cloned.1.call-update) | async-done | bytes 16777232 | tf_op jit(solution)/shard_map/all_gather | solution.py:22
  488.4 127.3 %all-gather.10.cloned.1.call-done = f32[256,128,128]{2,1,0:T(8,128)} async-done(((f32[16,128,128]{2,1,0:T(8,128)}), f32[256,128,128]{2,1,0:T(8,128)}) %all-gather.10.cloned.1.call-update) | async-done | bytes 16777232 | tf_op jit(solution)/shard_map/all_gather | solution.py:22
  615.9 80.2 %while.29 = (s32[]{:T(128)}, f32[16,128,128]{2,1,0:T(8,128)S(1)}, f32[16,128,128]{2,1,0:T(8,128)S(1)}, s32[]{:T(128)}, f32[16,16,128,128]{3,2,1,0:T(8,128)}, /*i...) while((s32[]{:T(128)}, f32[16,128,128]{2,1,0:T(8,128)S(1)}, ...), condition=%wide.region_6.7_spmd, body=%wide.region_5.6_spmd.sunk | while | flops 805568512 | bytes 11535499 | solution.py:30
  616.1 2.8 convolution_add_fusion.8
  653.5 2.7 convolution_add_fusion.8
  658.8 2.8 convolution_add_fusion.8
  680.2 2.7 convolution_add_fusion.8
  (182 shorter events, 138.0 us)
Async XLA Ops:
  6.5 1.2 copy-start
  6.5 1.2 copy-start.9
  6.5 1.7 copy-start.13
  6.5 3.1 copy-start.10
  6.5 228.9 %all-gather.6.cloned.1.call-start = ((), (), s32[]{:S(2)}) async-start(), calls=%async_computation | async-start | bytes 18874368 | tf_op jit(solution)/shard_map/all_gather | solution.py:151
  7.3 481.1 %all-gather.8.cloned.1.call-start = ((), (), s32[]{:S(2)}) async-start(), calls=%async_computation.1 | async-start | bytes 17825792 | tf_op jit(solution)/shard_map/all_gather | solution.py:22
  9.7 239.8 %copy-start.11 = (bf16[3,4096]{1,0:T(4,128)(2,1)S(1)}, bf16[3,4096]{1,0:T(4,128)(2,1)}, u32[]{:S(2)}) copy-start(bf16[3,4096]{1,0:T(4,128)(2,1)} %param.20) | copy-start | bytes 73732
  244.5 5.0 collective-permute-start
  257.3 3.5 copy-start.12
  320.0 1.6 copy-start.5
  320.1 3.4 copy-start.2
  330.0 1.6 copy-start.5
  330.1 3.4 copy-start.2
  340.0 1.6 copy-start.5
  340.1 3.4 copy-start.2
  350.0 1.6 copy-start.5
  350.1 3.4 copy-start.2
  360.0 1.3 copy-start.4
  360.9 254.8 %all-gather.10.cloned.1.call-start = ((), (), s32[]{:S(2)}) async-start(), calls=%async_computation.2 | async-start | bytes 17825792 | tf_op jit(solution)/shard_map/all_gather | solution.py:22
  615.9 80.2 %copy-start.8 = (f32[16,128,128]{2,1,0:T(8,128)S(1)}, f32[16,128,128]{2,1,0:T(8,128)}, u32[]{:S(2)}) copy-start(f32[16,128,128]{2,1,0:T(8,128)} %param.21) | copy-start | bytes 3145732
  696.2 1.6 copy-start.6
  696.2 2.2 copy-start.7
  698.4 2.5 copy-start.14
  701.0 2.7 copy-start.1
  (2 other events, 1.8 us)
Sparse Core Ops, SparseCore 0:
  9.4 226.0 all-gather.5
  361.1 127.2 all-gather.7
  490.6 125.0 all-gather.9
where the time goes:
time: 716 us; the launch traced here: 710 us
  waiting for transfers between devices  484 us (68%)
  matrix products  184 us (26%)
  local copies, waits for them, and re-layouts  16.5 us (2%)
  between operations  13.8 us (2%)
  other arithmetic  9.23 us (1%)
    all_gather x2, waiting for transfers between devices, entering(): gathered = jax.tree.map(lambda a: lax.all_gather(a, axis), part)  254 us
    all_gather x1, waiting for transfers between devices, shards(): lax.all_gather(qkv_weight, 'fsdp', axis=1, tiled=True)  226 us
    dot_general x15, matrix products, compose(): jnp.einsum('zom,zmg->zog', latter_piece[0], former_piece[1], precision=ex...  40.7 us
    dot_general x15, matrix products, compose(): jnp.einsum('hkj,hjm->hkm', latter_piece[0], former_piece[0], precision=ex...  36.3 us
  transfers between devices with their start and end apart: 4, of which 4 were waited for; matrix products, arithmetic and copies ran while one was open for 0% of the time, Pallas kernels for 0%

commit v1 on v0

--- a/solution.py
+++ b/solution.py
@@ -9,6 +9,24 @@
 DV = 128
 SPAN = 64
 exact_product = lax.Precision.HIGHEST
+
+
+def ring_gather(value, axis, dim):
+    ways, here, step = (lax.axis_size(axis), lax.axis_index(axis), value.shape[dim])
+    lengths = [n * ways if d == dim else n for d, n in enumerate(value.shape)]
+    full = lax.dynamic_update_slice_in_dim(
+        jnp.zeros(lengths, value.dtype), value, here * step, axis=dim
+    )
+    going_up = going_down = value
+    for far in range(1, ways // 2 + 1):
+        going_up = lax.ppermute(going_up, axis, [(d, (d + 1) % ways) for d in range(ways)])
+        full = lax.dynamic_update_slice_in_dim(full, going_up, (here - far) % ways * step, axis=dim)
+        if 2 * far < ways:
+            going_down = lax.ppermute(going_down, axis, [(d, (d - 1) % ways) for d in range(ways)])
+            full = lax.dynamic_update_slice_in_dim(
+                full, going_down, (here + far) % ways * step, axis=dim
+            )
+    return full
 
 
 def shifted(array, axis, by):
@@ -147,9 +165,7 @@
     window_entry_state,
 ):
     mixed_qkv = jnp.dot(
-        hidden_in,
-        lax.all_gather(qkv_weight, "fsdp", axis=1, tiled=True),
-        preferred_element_type=jnp.float32,
+        hidden_in, ring_gather(qkv_weight, "fsdp", 1), preferred_element_type=jnp.float32
     ).astype(jnp.bfloat16)
     gate_logits = jnp.dot(hidden_in, ab_weight, preferred_element_type=jnp.float32)
     tail_rows = previous_tail.shape[0]

time: 716 us -> 807 us (1.13)
  waiting for transfers between devices: 484 us -> 554 us
  local copies, waits for them, and re-layouts: 16.5 us -> 25 us
    ppermute x0 -> x7, waiting for transfers between devices: none -> 293 us  [the longest x4 293 us: ring_gather(): lax.ppermute(going_up, axis, [(d, (d + 1) % ways) for d in range(ways)])]
    all_gather x1 -> x0, waiting for transfers between devices: 226 us -> none  [shards(): lax.all_gather(qkv_weight, 'fsdp', axis=1, tiled=True)]
    dynamic_update_slice x0 -> x8, local copies, waits for them, and re-layouts: none -> 12.3 us  [the longest x4 6.15 us: ring_gather(): lax.dynamic_update_slice_in_dim(full, going_up, (here - far) % ways * ste...]
  transfers between devices with their start and end apart: 4 -> 10, of which waited for: 4 -> 8; matrix products, arithmetic and copies ran while one was open for 0% -> 2% of each run, Pallas kernels for 0% -> 0%
where the time goes in v1:
time: 807 us; the launch traced here: 799 us
  waiting for transfers between devices  554 us (69%)
  matrix products  188 us (23%)
  local copies, waits for them, and re-layouts  25 us (3%)
  between operations  14.4 us (2%)
  other arithmetic  10.7 us (1%)
    ppermute x4, waiting for transfers between devices, ring_gather(): lax.ppermute(going_up, axis, [(d, (d + 1) % ways) for d in range(ways)])  293 us
    all_gather x2, waiting for transfers between devices, entering(): gathered = jax.tree.map(lambda a: lax.all_gather(a, axis), part)  257 us
    dot_general x15, matrix products, compose(): jnp.einsum('zom,zmg->zog', latter_piece[0], former_piece[1], precision=ex...  41.3 us
    dot_general x15, matrix products, compose(): jnp.einsum('hkj,hjm->hkm', latter_piece[0], former_piece[0], precision=ex...  35.7 us
  transfers between devices with their start and end apart: 10, of which 8 were waited for; matrix products, arithmetic and copies ran while one was open for 2% of the time, Pallas kernels for 0%

profile of v1, /device:TPU:31, one launch (start us, length us, event | category | flops | bytes accessed | tf_op | source)
XLA Modules:
  0.0 799.3 jit_solution(7994593494712777607)
XLA Ops:
  8.0 90.2 %collective-permute-done = bf16[2048,512]{1,0:T(8,128)(2,1)S(1)} collective-permute-done((bf16[2048,512]{1,0:T(8,128)(2,1)}, bf16[2048,512]{1,0:T(8,128)(2,1)S(1)}, u32[]{:S(2)}, u32[]{:S(2)}) %collective-permute-start) | collective-permute-done | bytes 2097184 | tf_op jit(solution)/shard_map/ppermute | solution.py:22
  100.5 88.3 %collective-permute-done.2 = bf16[2048,512]{1,0:T(8,128)(2,1)} collective-permute-done((bf16[2048,512]{1,0:T(8,128)(2,1)S(1)}, bf16[2048,512]{1,0:T(8,128)(2,1)}, u32[]{:S(2)}, u32[]{:S(2)}) %collective-permute-start.2) | collective-permute-done | bytes 2097184 | tf_op jit(solution)/shard_map/ppermute | solution.py:22
  195.5 83.2 %collective-permute-done.4 = bf16[2048,512]{1,0:T(8,128)(2,1)} collective-permute-done((bf16[2048,512]{1,0:T(8,128)(2,1)}, bf16[2048,512]{1,0:T(8,128)(2,1)}, u32[]{:S(2)}, u32[]{:S(2)}) %collective-permute-start.4) | collective-permute-done | bytes 2097184 | tf_op jit(solution)/shard_map/ppermute | solution.py:22
  291.3 31.5 %collective-permute-done.6 = bf16[2048,512]{1,0:T(8,128)(2,1)} collective-permute-done((bf16[2048,512]{1,0:T(8,128)(2,1)}, bf16[2048,512]{1,0:T(8,128)(2,1)}, u32[]{:S(2)}, u32[]{:S(2)}) %collective-permute-start.6) | collective-permute-done | bytes 2097184 | tf_op jit(solution)/shard_map/ppermute | solution.py:22
  324.7 4.7 fusion.31
  332.0 3.0 collective-permute-done.7
  336.4 3.0 divide_multiply_fusion
  342.6 3.5 fusion.46
  346.1 3.6 select_multiply_fusion
  374.7 4.7 fusion.35
  379.4 3.6 fusion.48
  383.0 3.9 fusion.41
  387.0 8.9 %fusion.47 = f32[4,16,128,128]{3,2,1,0:T(8,128)} fusion(f32[4,16,64,256]{3,2,1,0:T(8,128)S(1)} %fusion.35, f32[4,64,16,128]{3,1,0,2:T(8,128)S(1)} %bitcast.168, f32[4,16,64]{2,1,0:T(8,128)S(1)} %get-tuple-element.163), kind=kOutput, calls=%fused_computation.69 | convolution fusion | flops 805830656 | bytes 8421376 | tf_op jit(solution)/shard_map/...ck,...cv->...kv/dot_general | solution.py:130
  395.9 9.4 %multiply_subtract_fusion = f32[4,16,128,128]{3,2,1,0:T(8,128)} fusion(f32[128,128]{1,0:T(8,128)S(1)} %fusion.77, f32[4,16]{1,0:T(4,128)S(1)} %exp.36, f32[4,16,64,256]{3,2,1,0:T(8,128)S(1)} %fusion.35, f32[4,64,16,128]{3,1,0,2:T(8,128)S(1)} %bitcast.169, f32[4,16,64]{2,1,0:T(8,128)S(1)} %get-tuple-element.163), kind=kOutput, calls=%fused_computation.49 | convolution fusion | flops 807927808 | bytes 8488960 | tf_op jit(solution)/shard_map/...ck,...cj->...kj/dot_general | solution.py:127
  405.4 39.6 %while.30 = (s32[]{:T(128)}, f32[16,128,128]{2,1,0:T(8,128)S(1)}, f32[16,128,128]{2,1,0:T(8,128)S(1)}, f32[4,16,64,128]{3,2,0,1:T(8,128)}, f32[4,16,64,128]{3,2,...) while((s32[]{:T(128)}, f32[16,128,128]{2,1,0:T(8,128)S(1)}, ...), condition=%wide.region_4.5_spmd.clone, body=%wide.region_3.4_spmd.clone.sunk | while | flops 1208877056 | bytes 33033364 | solution.py:198
  405.5 3.2 fusion.158
  415.4 3.2 fusion.158
  421.1 2.9 fusion.157
  425.3 3.2 fusion.158
  435.2 3.2 fusion.158
  446.7 129.5 %all-gather.5.cloned.1.call-done = f32[256,128,128]{2,1,0:T(8,128)} async-done(((f32[16,128,128]{2,1,0:T(8,128)}), f32[256,128,128]{2,1,0:T(8,128)}) %all-gather.5.cloned.1.call-update) | async-done | bytes 16777232 | tf_op jit(solution)/shard_map/all_gather | solution.py:40
  576.2 127.3 %all-gather.7.cloned.1.call-done = f32[256,128,128]{2,1,0:T(8,128)} async-done(((f32[16,128,128]{2,1,0:T(8,128)}), f32[256,128,128]{2,1,0:T(8,128)}) %all-gather.7.cloned.1.call-update) | async-done | bytes 16777232 | tf_op jit(solution)/shard_map/all_gather | solution.py:40
  703.8 80.1 %while.29 = (s32[]{:T(128)}, f32[16,128,128]{2,1,0:T(8,128)S(1)}, f32[16,128,128]{2,1,0:T(8,128)S(1)}, s32[]{:T(128)}, f32[16,16,128,128]{3,2,1,0:T(8,128)}, /*i...) while((s32[]{:T(128)}, f32[16,128,128]{2,1,0:T(8,128)S(1)}, ...), condition=%wide.region_6.7_spmd, body=%wide.region_5.6_spmd.sunk | while | flops 805568512 | bytes 11535491 | solution.py:48
  785.5 4.0 multiply_reduce_fusion
  (186 shorter events, 165.3 us)
Async XLA Ops:
  6.5 182.9 %copy-start = (bf16[256,2048]{1,0:T(8,128)(2,1)S(1)}, bf16[256,2048]{1,0:T(8,128)(2,1)}, u32[]{:S(2)}) copy-start(bf16[256,2048]{1,0:T(8,128)(2,1)} %param.13) | copy-start | bytes 3145732
  6.5 569.7 %all-gather.5.cloned.1.call-start = ((), (), s32[]{:S(2)}) async-start(), calls=%async_computation | async-start | bytes 17825792 | tf_op jit(solution)/shard_map/all_gather | solution.py:40
  6.5 91.7 %collective-permute-start = (bf16[2048,512]{1,0:T(8,128)(2,1)}, bf16[2048,512]{1,0:T(8,128)(2,1)S(1)}, u32[]{:S(2)}, u32[]{:S(2)}) collective-permute-start(bf16[2048,512]{1,0:T(8,128)(2,1)} %param.14), channel_id=1, source_target_pairs={{0,1},{1,2},{2,3},{3,4},{4,5},{5,6},{6,7},{7,0},{8,9},{9,10},{10,1... | collective-permute-start | bytes 6291464 | tf_op jit(solution)/shard_map/ppermute | solution.py:22
  6.5 91.7 %collective-permute-start.1 = (bf16[2048,512]{1,0:T(8,128)(2,1)}, bf16[2048,512]{1,0:T(8,128)(2,1)}, u32[]{:S(2)}, u32[]{:S(2)}) collective-permute-start(bf16[2048,512]{1,0:T(8,128)(2,1)} %param.14), channel_id=1, source_target_pairs={{0,7},{1,0},{2,1},{3,2},{4,3},{5,4},{6,5},{7,6},{8,15},{9,8},{10,9... | collective-permute-start | bytes 6291464 | tf_op jit(solution)/shard_map/ppermute | solution.py:25
  98.2 90.6 %collective-permute-start.2 = (bf16[2048,512]{1,0:T(8,128)(2,1)S(1)}, bf16[2048,512]{1,0:T(8,128)(2,1)}, u32[]{:S(2)}, u32[]{:S(2)}) collective-permute-start(bf16[2048,512]{1,0:T(8,128)(2,1)S(1)} %collective-permute-done), channel_id=1, source_target_pairs={{0,1},{1,2},{2,3},{3,4},{4,5},{5,6},{6,7},{7,0},{8,9},{9,10},{10,1... | collective-permute-start | bytes 6291464 | tf_op jit(solution)/shard_map/ppermute | solution.py:22
  98.3 95.6 %collective-permute-start.3 = (bf16[2048,512]{1,0:T(8,128)(2,1)}, bf16[2048,512]{1,0:T(8,128)(2,1)}, u32[]{:S(2)}, u32[]{:S(2)}) collective-permute-start(bf16[2048,512]{1,0:T(8,128)(2,1)} %collective-permute-done.1), channel_id=1, source_target_pairs={{0,7},{1,0},{2,1},{3,2},{4,3},{5,4},{6,5},{7,6},{8,15},{9,8},{10,9... | collective-permute-start | bytes 6291464 | tf_op jit(solution)/shard_map/ppermute | solution.py:25
  188.8 89.9 %collective-permute-start.4 = (bf16[2048,512]{1,0:T(8,128)(2,1)}, bf16[2048,512]{1,0:T(8,128)(2,1)}, u32[]{:S(2)}, u32[]{:S(2)}) collective-permute-start(bf16[2048,512]{1,0:T(8,128)(2,1)} %collective-permute-done.2), channel_id=1, source_target_pairs={{0,1},{1,2},{2,3},{3,4},{4,5},{5,6},{6,7},{7,0},{8,9},{9,10},{10,1... | collective-permute-start | bytes 6291464 | tf_op jit(solution)/shard_map/ppermute | solution.py:22
  193.9 95.5 %collective-permute-start.5 = (bf16[2048,512]{1,0:T(8,128)(2,1)}, bf16[2048,512]{1,0:T(8,128)(2,1)}, u32[]{:S(2)}, u32[]{:S(2)}) collective-permute-start(bf16[2048,512]{1,0:T(8,128)(2,1)} %collective-permute-done.3), channel_id=1, source_target_pairs={{0,7},{1,0},{2,1},{3,2},{4,3},{5,4},{6,5},{7,6},{8,15},{9,8},{10,9... | collective-permute-start | bytes 6291464 | tf_op jit(solution)/shard_map/ppermute | solution.py:25
  278.7 44.0 %collective-permute-start.6 = (bf16[2048,512]{1,0:T(8,128)(2,1)}, bf16[2048,512]{1,0:T(8,128)(2,1)}, u32[]{:S(2)}, u32[]{:S(2)}) collective-permute-start(bf16[2048,512]{1,0:T(8,128)(2,1)} %collective-permute-done.4), channel_id=1, source_target_pairs={{0,1},{1,2},{2,3},{3,4},{4,5},{5,6},{6,7},{7,0},{8,9},{9,10},{10,1... | collective-permute-start | bytes 6291464 | tf_op jit(solution)/shard_map/ppermute | solution.py:22
  278.9 1.9 copy-start.6
  324.7 10.3 %copy-start.8 = (bf16[3,4096]{1,0:T(4,128)(2,1)S(1)}, bf16[3,4096]{1,0:T(4,128)(2,1)}, u32[]{:S(2)}) copy-start(bf16[3,4096]{1,0:T(4,128)(2,1)} %param.20) | copy-start | bytes 73732
  330.1 5.0 collective-permute-start.7
  342.6 3.5 copy-start.9
  405.4 3.3 copy-start.2
  415.3 3.3 copy-start.2
  425.2 3.3 copy-start.2
  435.1 3.3 copy-start.2
  445.0 1.0 copy-start.3
  445.0 1.3 copy-start.4
  446.0 257.6 %all-gather.7.cloned.1.call-start = ((), (), s32[]{:S(2)}) async-start(), calls=%async_computation.1 | async-start | bytes 17825792 | tf_op jit(solution)/shard_map/all_gather | solution.py:40
  703.8 80.1 %copy-start.7 = (f32[16,128,128]{2,1,0:T(8,128)S(1)}, f32[16,128,128]{2,1,0:T(8,128)}, u32[]{:S(2)}) copy-start(f32[16,128,128]{2,1,0:T(8,128)} %param.21) | copy-start | bytes 3145732
  783.9 1.6 copy-start.5
  785.5 4.1 copy-start.10
  789.5 2.7 copy-start.1
Sparse Core Ops, SparseCore 0:
  446.1 130.1 all-gather.4
  578.4 125.0 all-gather.6
